TPU v7x, 256 devices: a whole 4x4x8 slice. The times are simulated.
256 devices in a mesh: section: 4 (over x), col: 16 (over z_hi, y), dist: 4 (over z_lo, core).
Axes of the slice: x: 4, y: 4, z: 8 (z_hi: 4, z_lo: 2; z = z_hi * 2 + z_lo), core: 2. Of those that a mesh axis runs over, the one named last changes fastest.
Arguments:
- activations: bfloat16 [4, 1024, 14336], P('section', 'dist', 'col'), may hold values from -24 to 24
- out_grads: bfloat16 [4, 1024, 8192], P('section', 'dist', 'col'), may hold values from -24 to 24
- assign: int32 [9, 4], replicated, may hold values from 0 to 3, each once within a row
- act_old: bfloat16 [4, 9, 896, 14336], P('section', None, 'dist', 'col'), may hold values from -3 to 3
- grad_old: bfloat16 [4, 9, 512, 8192], P('section', None, 'dist', 'col'), may hold values from -3 to 3
Outputs:
- act_new: bfloat16 [4, 9, 896, 14336], P('section', None, 'dist', 'col')
- grad_new: bfloat16 [4, 9, 512, 8192], P('section', None, 'dist', 'col')
Inputs may be any that keep to these rules, and one draw needn't show every extreme that they name: Each row of assign is a permutation of 0 to 4 - 1.
All inputs are finite; a program needn't handle non-finite values.
Results may differ from a plain program's by a relative error of at most 0.001.
Values may be sent and summed in bfloat16 or wider, within the bound.
A program may use at most 128 MiB of HBM per device.

v0:
```python
import jax
import jax.numpy as jnp
from jax import lax
from jax.sharding import PartitionSpec as P

ema_decay = 0.75


def shifted(shard, axis, by):
    peers = lax.axis_size(axis)
    return lax.ppermute(shard, axis, [(i, (i + by) % peers) for i in range(peers)])


def blend(product, old_blocks, tokens):
    return (
        ema_decay * old_blocks.astype(jnp.float32) + (1.0 - ema_decay) * (product / tokens)
    ).astype(jnp.bfloat16)


def reorder(block, perm_row, act_width, n_dist):
    height = block.shape[0]
    act_part = block[:, :act_width].reshape(height, n_dist, act_width // n_dist)
    grad_part = block[:, act_width:].reshape(height, n_dist, (block.shape[1] - act_width) // n_dist)
    act_part = jnp.take(act_part, perm_row, axis=1)
    grad_part = jnp.take(grad_part, perm_row, axis=1)
    return jnp.concatenate([act_part, grad_part], 2).reshape(height, block.shape[1])


def on_device(activations, out_grads, assign, act_old, grad_old):
    n_dist = lax.axis_size("dist")
    act_rows = activations[0]
    act_width = act_rows.shape[1]
    act_strip = act_width // n_dist
    grad_rows = shifted(out_grads[0], "section", -1)
    own_act = lax.all_gather(act_rows, "dist", axis=0, tiled=True)
    own_grad = lax.all_gather(grad_rows, "dist", axis=0, tiled=True)
    tokens = own_act.shape[0]
    dists = assign.shape[0]
    joined = jnp.concatenate([act_rows, grad_rows], 1)

    def advance(carry, unused):
        moved = shifted(carry, "col", -1)
        return (moved, moved)

    unused_last, later = lax.scan(advance, joined, None, length=dists - 1)
    stacked = jnp.concatenate([joined[None], later], 0)

    def one_distance(counter, inputs):
        block, perm_row, old_act_block, old_grad_block = inputs
        sent = reorder(block, perm_row, act_width, n_dist)
        received = lax.all_to_all(sent, "dist", split_axis=1, concat_axis=0, tiled=True)
        act_product = lax.dot_general(
            received[:, :act_strip],
            own_act,
            (((0,), (0,)), ((), ())),
            preferred_element_type=jnp.float32,
        )
        grad_product = lax.dot_general(
            received[:, act_strip:],
            own_grad,
            (((0,), (0,)), ((), ())),
            preferred_element_type=jnp.float32,
        )
        return (
            counter,
            (
                blend(act_product, old_act_block, tokens),
                blend(grad_product, old_grad_block, tokens),
            ),
        )

    counter_end, (act_new, grad_new) = lax.scan(
        one_distance, jnp.zeros((), jnp.int32), (stacked, assign, act_old[0], grad_old[0])
    )
    return (act_new[None], grad_new[None])


def solution(mesh):
    return jax.shard_map(
        on_device,
        mesh=mesh,
        in_specs=(
            P("section", "dist", "col"),
            P("section", "dist", "col"),
            P(),
            P("section", None, "dist", "col"),
            P("section", None, "dist", "col"),
        ),
        out_specs=(P("section", None, "dist", "col"), P("section", None, "dist", "col")),
        check_vma=False,
    )
```

profile of v0, /device:TPU:247, one launch (start us, length us, event | category | flops | bytes accessed | tf_op | source)
XLA Modules:
  0.0 549.7 jit_solution(9437730399843134604)
XLA Ops:
  7.8 8.0 %collective-permute-done.1 = bf16[256,512]{1,0:T(8,128)(2,1)S(1)} collective-permute-done((bf16[256,512]{1,0:T(8,128)(2,1)}, bf16[256,512]{1,0:T(8,128)(2,1)S(1)}, u32[]{:S(2)}, u32[]{:S(2)}) %collective-permute-start.1) | collective-permute-done | bytes 262176 | tf_op jit(solution)/shard_map/ppermute | solution.py:11
  20.9 307.5 %while.27 = (s32[]{:T(128)}, bf16[256,1408]{1,0:T(8,128)(2,1)S(1)}, bf16[8,256,1408]{1,2,0:T(8,128)(2,1)}, s32[]{:T(128)}) while((s32[]{:T(128)}, bf16[256,1408]{1,0:T(8,128)(2,1)S(1)}, bf16[8,256,1408]{1,2,0:T(8,128)(2,1)}, s32[]{:T(128)}) %tuple.52), condition=%wide.region_1.2_spmd, body=%wide.region_0.1_spmd.sunk | while | flops 2 | bytes 7209065 | solution.py:45
  21.2 16.0 %collective-permute-done = bf16[256,1408]{1,0:T(8,128)(2,1)S(1)} collective-permute-done((bf16[256,1408]{1,0:T(8,128)(2,1)S(1)}, bf16[256,1408]{1,0:T(8,128)(2,1)S(1)}, u32[]{:S(2)}, u32[]{:S(2)}) %collective-permute-start) | collective-permute-done | bytes 720928 | tf_op jit(solution)/shard_map/while/body/eval_jaxpr/ppermute | solution.py:11
  38.7 74.4 %collective-permute-done = bf16[256,1408]{1,0:T(8,128)(2,1)S(1)} collective-permute-done((bf16[256,1408]{1,0:T(8,128)(2,1)S(1)}, bf16[256,1408]{1,0:T(8,128)(2,1)S(1)}, u32[]{:S(2)}, u32[]{:S(2)}) %collective-permute-start) | collective-permute-done | bytes 720928 | tf_op jit(solution)/shard_map/while/body/eval_jaxpr/ppermute | solution.py:11
  114.5 112.4 %collective-permute-done = bf16[256,1408]{1,0:T(8,128)(2,1)S(1)} collective-permute-done((bf16[256,1408]{1,0:T(8,128)(2,1)S(1)}, bf16[256,1408]{1,0:T(8,128)(2,1)S(1)}, u32[]{:S(2)}, u32[]{:S(2)}) %collective-permute-start) | collective-permute-done | bytes 720928 | tf_op jit(solution)/shard_map/while/body/eval_jaxpr/ppermute | solution.py:11
  228.4 20.5 %collective-permute-done = bf16[256,1408]{1,0:T(8,128)(2,1)S(1)} collective-permute-done((bf16[256,1408]{1,0:T(8,128)(2,1)S(1)}, bf16[256,1408]{1,0:T(8,128)(2,1)S(1)}, u32[]{:S(2)}, u32[]{:S(2)}) %collective-permute-start) | collective-permute-done | bytes 720928 | tf_op jit(solution)/shard_map/while/body/eval_jaxpr/ppermute | solution.py:11
  250.3 19.6 %collective-permute-done = bf16[256,1408]{1,0:T(8,128)(2,1)S(1)} collective-permute-done((bf16[256,1408]{1,0:T(8,128)(2,1)S(1)}, bf16[256,1408]{1,0:T(8,128)(2,1)S(1)}, u32[]{:S(2)}, u32[]{:S(2)}) %collective-permute-start) | collective-permute-done | bytes 720928 | tf_op jit(solution)/shard_map/while/body/eval_jaxpr/ppermute | solution.py:11
  271.2 18.7 %collective-permute-done = bf16[256,1408]{1,0:T(8,128)(2,1)S(1)} collective-permute-done((bf16[256,1408]{1,0:T(8,128)(2,1)S(1)}, bf16[256,1408]{1,0:T(8,128)(2,1)S(1)}, u32[]{:S(2)}, u32[]{:S(2)}) %collective-permute-start) | collective-permute-done | bytes 720928 | tf_op jit(solution)/shard_map/while/body/eval_jaxpr/ppermute | solution.py:11
  291.3 17.7 %collective-permute-done = bf16[256,1408]{1,0:T(8,128)(2,1)S(1)} collective-permute-done((bf16[256,1408]{1,0:T(8,128)(2,1)S(1)}, bf16[256,1408]{1,0:T(8,128)(2,1)S(1)}, u32[]{:S(2)}, u32[]{:S(2)}) %collective-permute-start) | collective-permute-done | bytes 720928 | tf_op jit(solution)/shard_map/while/body/eval_jaxpr/ppermute | solution.py:11
  310.4 16.8 %collective-permute-done = bf16[256,1408]{1,0:T(8,128)(2,1)S(1)} collective-permute-done((bf16[256,1408]{1,0:T(8,128)(2,1)S(1)}, bf16[256,1408]{1,0:T(8,128)(2,1)S(1)}, u32[]{:S(2)}, u32[]{:S(2)}) %collective-permute-start) | collective-permute-done | bytes 720928 | tf_op jit(solution)/shard_map/while/body/eval_jaxpr/ppermute | solution.py:11
  328.5 5.9 %pad_maximum_fusion.1 = bf16[9,256,1408]{1,2,0:T(8,128)(2,1)} fusion(bf16[8,256,1408]{1,2,0:T(8,128)(2,1)} %get-tuple-element.157, bf16[1,256,1408]{1,2,0:T(8,128)(2,1)S(1)} %get-tuple-element.217), kind=kLoop, calls=%fused_computation.25 | loop fusion | flops 3244032 | bytes 12976128 | tf_op jit(solution)/shard_map/concatenate | solution.py:46
  334.4 208.5 %while.28 = (s32[]{:T(128)}, bf16[9,224,896]{2,1,0:T(8,128)(2,1)}, bf16[9,128,512]{2,1,0:T(8,128)(2,1)}, bf16[9,224,896]{2,1,0:T(8,128)(2,1)}, s32[9,4]{1,0:T(8,...) while((s32[]{:T(128)}, bf16[9,224,896]{2,1,0:T(8,128)(2,1)}, ...), condition=%wide.region_3.4_spmd, body=%wide.region_2.3_spmd.sunk | while | flops 548393984 | bytes 28070212 | solution.py:72
  338.3 8.6 %all-to-all-start = ((bf16[256,4,352]{0,2,1:T(8,128)(2,1)}), bf16[256,4,352]{0,2,1:T(8,128)(2,1)S(1)}, u32[]{:S(2)}, u32[]{:S(2)}) async-start(bf16[256,4,352]{0,2,1:T(8,128)(2,1)} %pad_maximum_fusion.4), calls=%async_computation | async-start | bytes 1441792 | tf_op jit(solution)/shard_map/while/body/eval_jaxpr/all_to_all | solution.py:51
  346.9 9.1 %all-to-all-done = bf16[256,4,352]{0,2,1:T(8,128)(2,1)S(1)} async-done(((bf16[256,4,352]{0,2,1:T(8,128)(2,1)}), bf16[256,4,352]{0,2,1:T(8,128)(2,1)S(1)}, u32[]{:S(2)}, u32[]{:S(2)}) %all-to-all-start) | async-done | bytes 720928 | tf_op jit(solution)/shard_map/while/body/eval_jaxpr/all_to_all | solution.py:51
  369.7 9.0 %all-to-all-done = bf16[256,4,352]{0,2,1:T(8,128)(2,1)S(1)} async-done(((bf16[256,4,352]{0,2,1:T(8,128)(2,1)}), bf16[256,4,352]{0,2,1:T(8,128)(2,1)S(1)}, u32[]{:S(2)}, u32[]{:S(2)}) %all-to-all-start) | async-done | bytes 720928 | tf_op jit(solution)/shard_map/while/body/eval_jaxpr/all_to_all | solution.py:51
  392.5 9.0 %all-to-all-done = bf16[256,4,352]{0,2,1:T(8,128)(2,1)S(1)} async-done(((bf16[256,4,352]{0,2,1:T(8,128)(2,1)}), bf16[256,4,352]{0,2,1:T(8,128)(2,1)S(1)}, u32[]{:S(2)}, u32[]{:S(2)}) %all-to-all-start) | async-done | bytes 720928 | tf_op jit(solution)/shard_map/while/body/eval_jaxpr/all_to_all | solution.py:51
  415.3 9.0 %all-to-all-done = bf16[256,4,352]{0,2,1:T(8,128)(2,1)S(1)} async-done(((bf16[256,4,352]{0,2,1:T(8,128)(2,1)}), bf16[256,4,352]{0,2,1:T(8,128)(2,1)S(1)}, u32[]{:S(2)}, u32[]{:S(2)}) %all-to-all-start) | async-done | bytes 720928 | tf_op jit(solution)/shard_map/while/body/eval_jaxpr/all_to_all | solution.py:51
  432.7 5.4 all-to-all-start
  438.1 9.0 %all-to-all-done = bf16[256,4,352]{0,2,1:T(8,128)(2,1)S(1)} async-done(((bf16[256,4,352]{0,2,1:T(8,128)(2,1)}), bf16[256,4,352]{0,2,1:T(8,128)(2,1)S(1)}, u32[]{:S(2)}, u32[]{:S(2)}) %all-to-all-start) | async-done | bytes 720928 | tf_op jit(solution)/shard_map/while/body/eval_jaxpr/all_to_all | solution.py:51
  460.9 9.0 %all-to-all-done = bf16[256,4,352]{0,2,1:T(8,128)(2,1)S(1)} async-done(((bf16[256,4,352]{0,2,1:T(8,128)(2,1)}), bf16[256,4,352]{0,2,1:T(8,128)(2,1)S(1)}, u32[]{:S(2)}, u32[]{:S(2)}) %all-to-all-start) | async-done | bytes 720928 | tf_op jit(solution)/shard_map/while/body/eval_jaxpr/all_to_all | solution.py:51
  483.7 9.0 %all-to-all-done = bf16[256,4,352]{0,2,1:T(8,128)(2,1)S(1)} async-done(((bf16[256,4,352]{0,2,1:T(8,128)(2,1)}), bf16[256,4,352]{0,2,1:T(8,128)(2,1)S(1)}, u32[]{:S(2)}, u32[]{:S(2)}) %all-to-all-start) | async-done | bytes 720928 | tf_op jit(solution)/shard_map/while/body/eval_jaxpr/all_to_all | solution.py:51
  501.2 5.4 all-to-all-start
  506.5 9.0 %all-to-all-done = bf16[256,4,352]{0,2,1:T(8,128)(2,1)S(1)} async-done(((bf16[256,4,352]{0,2,1:T(8,128)(2,1)}), bf16[256,4,352]{0,2,1:T(8,128)(2,1)S(1)}, u32[]{:S(2)}, u32[]{:S(2)}) %all-to-all-start) | async-done | bytes 720928 | tf_op jit(solution)/shard_map/while/body/eval_jaxpr/all_to_all | solution.py:51
  529.3 9.0 %all-to-all-done = bf16[256,4,352]{0,2,1:T(8,128)(2,1)S(1)} async-done(((bf16[256,4,352]{0,2,1:T(8,128)(2,1)}), bf16[256,4,352]{0,2,1:T(8,128)(2,1)S(1)}, u32[]{:S(2)}, u32[]{:S(2)}) %all-to-all-start) | async-done | bytes 720928 | tf_op jit(solution)/shard_map/while/body/eval_jaxpr/all_to_all | solution.py:51
  (235 shorter events, 123.7 us)
Async XLA Ops:
  7.2 327.2 %all-gather.4.cloned.1.call-start = ((), (), s32[]{:S(2)}) async-start(), calls=%async_computation.1 | async-start | bytes 1310720 | tf_op jit(solution)/shard_map/all_gather | solution.py:36
  7.2 8.7 %collective-permute-start.1 = (bf16[256,512]{1,0:T(8,128)(2,1)}, bf16[256,512]{1,0:T(8,128)(2,1)S(1)}, u32[]{:S(2)}, u32[]{:S(2)}) collective-permute-start(bf16[256,512]{1,0:T(8,128)(2,1)} %bitcast.85), channel_id=1, source_target_pairs={{0,192},{64,0},{128,64},{192,128},{1,193},{65,1},{129,65},{193,129... | collective-permute-start | bytes 786440 | tf_op jit(solution)/shard_map/ppermute | solution.py:11
  16.6 317.7 %all-gather.6.cloned.1.call-start = ((), (), s32[]{:S(2)}) async-start(), calls=%async_computation.2 | async-start | bytes 2293760 | tf_op jit(solution)/shard_map/all_gather | solution.py:35
  20.9 16.3 %collective-permute-start = (bf16[256,1408]{1,0:T(8,128)(2,1)S(1)}, bf16[256,1408]{1,0:T(8,128)(2,1)S(1)}, u32[]{:S(2)}, u32[]{:S(2)}) collective-permute-start(bf16[256,1408]{1,0:T(8,128)(2,1)S(1)} %get-tuple-element.298), channel_id=1, source_target_pairs={{0,60},{4,0},{8,4},{12,8},{16,12},{20,16},{24,20},{28,24},{32,28},... | collective-permute-start | bytes 2162696 | tf_op jit(solution)/shard_map/while/body/eval_jaxpr/ppermute | solution.py:11
  38.5 74.7 %collective-permute-start = (bf16[256,1408]{1,0:T(8,128)(2,1)S(1)}, bf16[256,1408]{1,0:T(8,128)(2,1)S(1)}, u32[]{:S(2)}, u32[]{:S(2)}) collective-permute-start(bf16[256,1408]{1,0:T(8,128)(2,1)S(1)} %get-tuple-element.298), channel_id=1, source_target_pairs={{0,60},{4,0},{8,4},{12,8},{16,12},{20,16},{24,20},{28,24},{32,28},... | collective-permute-start | bytes 2162696 | tf_op jit(solution)/shard_map/while/body/eval_jaxpr/ppermute | solution.py:11
  114.5 112.5 %collective-permute-start = (bf16[256,1408]{1,0:T(8,128)(2,1)S(1)}, bf16[256,1408]{1,0:T(8,128)(2,1)S(1)}, u32[]{:S(2)}, u32[]{:S(2)}) collective-permute-start(bf16[256,1408]{1,0:T(8,128)(2,1)S(1)} %get-tuple-element.298), channel_id=1, source_target_pairs={{0,60},{4,0},{8,4},{12,8},{16,12},{20,16},{24,20},{28,24},{32,28},... | collective-permute-start | bytes 2162696 | tf_op jit(solution)/shard_map/while/body/eval_jaxpr/ppermute | solution.py:11
  228.3 20.5 %collective-permute-start = (bf16[256,1408]{1,0:T(8,128)(2,1)S(1)}, bf16[256,1408]{1,0:T(8,128)(2,1)S(1)}, u32[]{:S(2)}, u32[]{:S(2)}) collective-permute-start(bf16[256,1408]{1,0:T(8,128)(2,1)S(1)} %get-tuple-element.298), channel_id=1, source_target_pairs={{0,60},{4,0},{8,4},{12,8},{16,12},{20,16},{24,20},{28,24},{32,28},... | collective-permute-start | bytes 2162696 | tf_op jit(solution)/shard_map/while/body/eval_jaxpr/ppermute | solution.py:11
  250.2 19.7 %collective-permute-start = (bf16[256,1408]{1,0:T(8,128)(2,1)S(1)}, bf16[256,1408]{1,0:T(8,128)(2,1)S(1)}, u32[]{:S(2)}, u32[]{:S(2)}) collective-permute-start(bf16[256,1408]{1,0:T(8,128)(2,1)S(1)} %get-tuple-element.298), channel_id=1, source_target_pairs={{0,60},{4,0},{8,4},{12,8},{16,12},{20,16},{24,20},{28,24},{32,28},... | collective-permute-start | bytes 2162696 | tf_op jit(solution)/shard_map/while/body/eval_jaxpr/ppermute | solution.py:11
  271.1 18.7 %collective-permute-start = (bf16[256,1408]{1,0:T(8,128)(2,1)S(1)}, bf16[256,1408]{1,0:T(8,128)(2,1)S(1)}, u32[]{:S(2)}, u32[]{:S(2)}) collective-permute-start(bf16[256,1408]{1,0:T(8,128)(2,1)S(1)} %get-tuple-element.298), channel_id=1, source_target_pairs={{0,60},{4,0},{8,4},{12,8},{16,12},{20,16},{24,20},{28,24},{32,28},... | collective-permute-start | bytes 2162696 | tf_op jit(solution)/shard_map/while/body/eval_jaxpr/ppermute | solution.py:11
  291.2 17.8 %collective-permute-start = (bf16[256,1408]{1,0:T(8,128)(2,1)S(1)}, bf16[256,1408]{1,0:T(8,128)(2,1)S(1)}, u32[]{:S(2)}, u32[]{:S(2)}) collective-permute-start(bf16[256,1408]{1,0:T(8,128)(2,1)S(1)} %get-tuple-element.298), channel_id=1, source_target_pairs={{0,60},{4,0},{8,4},{12,8},{16,12},{20,16},{24,20},{28,24},{32,28},... | collective-permute-start | bytes 2162696 | tf_op jit(solution)/shard_map/while/body/eval_jaxpr/ppermute | solution.py:11
  310.3 16.9 %collective-permute-start = (bf16[256,1408]{1,0:T(8,128)(2,1)S(1)}, bf16[256,1408]{1,0:T(8,128)(2,1)S(1)}, u32[]{:S(2)}, u32[]{:S(2)}) collective-permute-start(bf16[256,1408]{1,0:T(8,128)(2,1)S(1)} %get-tuple-element.298), channel_id=1, source_target_pairs={{0,60},{4,0},{8,4},{12,8},{16,12},{20,16},{24,20},{28,24},{32,28},... | collective-permute-start | bytes 2162696 | tf_op jit(solution)/shard_map/while/body/eval_jaxpr/ppermute | solution.py:11
  336.4 19.7 %copy-start.1 = (bf16[1024,896]{1,0:T(8,128)(2,1)S(1)}, bf16[1024,896]{1,0:T(8,128)(2,1)}, u32[]{:S(2)}) copy-start(bf16[1024,896]{1,0:T(8,128)(2,1)} %get-tuple-element.331) | copy-start | bytes 5505028 | tf_op jit(solution)/shard_map/while
  338.3 17.7 %all-to-all-start = ((bf16[256,4,352]{0,2,1:T(8,128)(2,1)}), bf16[256,4,352]{0,2,1:T(8,128)(2,1)S(1)}, u32[]{:S(2)}, u32[]{:S(2)}) async-start(bf16[256,4,352]{0,2,1:T(8,128)(2,1)} %pad_maximum_fusion.4), calls=%async_computation | async-start | bytes 1441792 | tf_op jit(solution)/shard_map/while/body/eval_jaxpr/all_to_all | solution.py:51
  364.4 14.4 %all-to-all-start = ((bf16[256,4,352]{0,2,1:T(8,128)(2,1)}), bf16[256,4,352]{0,2,1:T(8,128)(2,1)S(1)}, u32[]{:S(2)}, u32[]{:S(2)}) async-start(bf16[256,4,352]{0,2,1:T(8,128)(2,1)} %pad_maximum_fusion.4), calls=%async_computation | async-start | bytes 1441792 | tf_op jit(solution)/shard_map/while/body/eval_jaxpr/all_to_all | solution.py:51
  385.2 16.4 %copy-start.1 = (bf16[1024,896]{1,0:T(8,128)(2,1)S(1)}, bf16[1024,896]{1,0:T(8,128)(2,1)}, u32[]{:S(2)}) copy-start(bf16[1024,896]{1,0:T(8,128)(2,1)} %get-tuple-element.331) | copy-start | bytes 5505028 | tf_op jit(solution)/shard_map/while
  387.1 14.4 %all-to-all-start = ((bf16[256,4,352]{0,2,1:T(8,128)(2,1)}), bf16[256,4,352]{0,2,1:T(8,128)(2,1)S(1)}, u32[]{:S(2)}, u32[]{:S(2)}) async-start(bf16[256,4,352]{0,2,1:T(8,128)(2,1)} %pad_maximum_fusion.4), calls=%async_computation | async-start | bytes 1441792 | tf_op jit(solution)/shard_map/while/body/eval_jaxpr/all_to_all | solution.py:51
  409.9 14.4 %all-to-all-start = ((bf16[256,4,352]{0,2,1:T(8,128)(2,1)}), bf16[256,4,352]{0,2,1:T(8,128)(2,1)S(1)}, u32[]{:S(2)}, u32[]{:S(2)}) async-start(bf16[256,4,352]{0,2,1:T(8,128)(2,1)} %pad_maximum_fusion.4), calls=%async_computation | async-start | bytes 1441792 | tf_op jit(solution)/shard_map/while/body/eval_jaxpr/all_to_all | solution.py:51
  430.9 16.4 %copy-start.1 = (bf16[1024,896]{1,0:T(8,128)(2,1)S(1)}, bf16[1024,896]{1,0:T(8,128)(2,1)}, u32[]{:S(2)}) copy-start(bf16[1024,896]{1,0:T(8,128)(2,1)} %get-tuple-element.331) | copy-start | bytes 5505028 | tf_op jit(solution)/shard_map/while
  432.7 14.4 %all-to-all-start = ((bf16[256,4,352]{0,2,1:T(8,128)(2,1)}), bf16[256,4,352]{0,2,1:T(8,128)(2,1)S(1)}, u32[]{:S(2)}, u32[]{:S(2)}) async-start(bf16[256,4,352]{0,2,1:T(8,128)(2,1)} %pad_maximum_fusion.4), calls=%async_computation | async-start | bytes 1441792 | tf_op jit(solution)/shard_map/while/body/eval_jaxpr/all_to_all | solution.py:51
  455.6 14.4 %all-to-all-start = ((bf16[256,4,352]{0,2,1:T(8,128)(2,1)}), bf16[256,4,352]{0,2,1:T(8,128)(2,1)S(1)}, u32[]{:S(2)}, u32[]{:S(2)}) async-start(bf16[256,4,352]{0,2,1:T(8,128)(2,1)} %pad_maximum_fusion.4), calls=%async_computation | async-start | bytes 1441792 | tf_op jit(solution)/shard_map/while/body/eval_jaxpr/all_to_all | solution.py:51
  478.4 14.4 %all-to-all-start = ((bf16[256,4,352]{0,2,1:T(8,128)(2,1)}), bf16[256,4,352]{0,2,1:T(8,128)(2,1)S(1)}, u32[]{:S(2)}, u32[]{:S(2)}) async-start(bf16[256,4,352]{0,2,1:T(8,128)(2,1)} %pad_maximum_fusion.4), calls=%async_computation | async-start | bytes 1441792 | tf_op jit(solution)/shard_map/while/body/eval_jaxpr/all_to_all | solution.py:51
  499.3 16.4 %copy-start.1 = (bf16[1024,896]{1,0:T(8,128)(2,1)S(1)}, bf16[1024,896]{1,0:T(8,128)(2,1)}, u32[]{:S(2)}) copy-start(bf16[1024,896]{1,0:T(8,128)(2,1)} %get-tuple-element.331) | copy-start | bytes 5505028 | tf_op jit(solution)/shard_map/while
  501.2 14.4 %all-to-all-start = ((bf16[256,4,352]{0,2,1:T(8,128)(2,1)}), bf16[256,4,352]{0,2,1:T(8,128)(2,1)S(1)}, u32[]{:S(2)}, u32[]{:S(2)}) async-start(bf16[256,4,352]{0,2,1:T(8,128)(2,1)} %pad_maximum_fusion.4), calls=%async_computation | async-start | bytes 1441792 | tf_op jit(solution)/shard_map/while/body/eval_jaxpr/all_to_all | solution.py:51
  524.0 14.4 %all-to-all-start = ((bf16[256,4,352]{0,2,1:T(8,128)(2,1)}), bf16[256,4,352]{0,2,1:T(8,128)(2,1)S(1)}, u32[]{:S(2)}, u32[]{:S(2)}) async-start(bf16[256,4,352]{0,2,1:T(8,128)(2,1)} %pad_maximum_fusion.4), calls=%async_computation | async-start | bytes 1441792 | tf_op jit(solution)/shard_map/while/body/eval_jaxpr/all_to_all | solution.py:51
  (15 other events, 106.0 us)
Sparse Core Ops, SparseCore 0:
  16.7 24.3 all-gather.3
  42.9 79.8 all-gather.5
where the time goes:
time: 559 us; the launch traced here: 550 us
  waiting for transfers between devices  386 us (69%)
  starting transfers between devices  53.2 us (10%)
  local copies, waits for them, and re-layouts  39.5 us (7%)
  matrix products  39.3 us (7%)
  other arithmetic  16.3 us (3%)
  between operations  14.1 us (3%)
    ppermute x9, waiting for transfers between devices, shifted(): lax.ppermute(shard, axis, [(i, (i + by) % peers) for i in range(peers)])  304 us
    all_to_all x9, waiting for transfers between devices, one_distance(): lax.all_to_all(sent, 'dist', split_axis=1, concat_axis=0, tiled=True)  81.4 us
    all_to_all x9, starting transfers between devices, one_distance(): lax.all_to_all(sent, 'dist', split_axis=1, concat_axis=0, tiled=True)  51.5 us
    dot_general x9, matrix products, one_distance(): lax.dot_general(received[:, :act_strip], own_act, (((0,), (0,)), ((), ())...  22.4 us
    dot_general x9, matrix products, one_distance(): lax.dot_general(received[:, act_strip:], own_grad, (((0,), (0,)), ((), ()...  16.9 us
  transfers between devices with their start and end apart: 20, of which 18 were waited for; matrix products, arithmetic and copies ran while one was open for 4% of the time, Pallas kernels for 0%

commit v1 on v0

v1 whole, which is shorter than its diff:
```python
import functools
import jax
import jax.numpy as jnp
from jax import lax
from jax.experimental import pallas as pl
from jax.experimental.pallas import tpu as pltpu
from jax.sharding import PartitionSpec as P

ema_decay = 0.75
MESH = pl.DeviceIdType.MESH
NY = 4
NZ = 8
NX = 4


def kernel(
    act_ref, og_ref, assign_ref, olda_hbm, oldg_hbm, outa_hbm, outg_hbm,
    b0_a, p_a, c1_a, c2_a, c3_a, c4_a, oc0_a, ocp_a,
    b0_g, p_g, c1_g, c2_g, c3_g, c4_g, oc0_g, ocp_g,
    gbuf, stage_a, stage_g, recv_a, recv_g, olda, oldg,
    old_sem, out_sem, shift_sem, zsend, zrecv, ocsend, ocrecv, ysend, yrecv,
):
    x = lax.axis_index("section")
    c = lax.axis_index("col")
    q = lax.axis_index("dist")
    y, zh = lax.rem(c, NY), c // NY
    zl, k = q // 2, lax.rem(q, 2)
    z = 2 * zh + zl
    dists = olda.shape[0]
    parts = (
        dict(own=b0_a, p=p_a, c=(c1_a, c2_a, c3_a, c4_a), oc0=oc0_a, ocp=ocp_a,
             stage=stage_a, recv=recv_a, old=olda, out=outa_hbm, i=0),
        dict(own=b0_g, p=p_g, c=(c1_g, c2_g, c3_g, c4_g), oc0=oc0_g, ocp=ocp_g,
             stage=stage_g, recv=recv_g, old=oldg, out=outg_hbm, i=1),
    )

    def device(xx, zz, yy, kk):
        return (xx, (zz // 2) * NY + yy, lax.rem(zz, 2) * 2 + kk)

    z_down = device(x, lax.rem(z + NZ - 1, NZ), y, k)
    z_up = device(x, lax.rem(z + 1, NZ), y, k)
    twin = device(x, z, y, 1 - k)
    x_down = device(lax.rem(x + NX - 1, NX), z, y, k)
    x_up = device(lax.rem(x + 1, NX), z, y, k)

    old_copies = [
        pltpu.make_async_copy(olda_hbm, olda, old_sem.at[0]),
        pltpu.make_async_copy(oldg_hbm, oldg, old_sem.at[1]),
    ]

    barrier = pltpu.get_barrier_semaphore()
    greeted = [z_down, z_up, twin, x_down, x_up]
    for step in range(1, NY):
        for kk in range(2):
            greeted.append(device(x, z, lax.rem(y + step, NY), kk))
    for other in greeted:
        pl.semaphore_signal(barrier, inc=1, device_id=other, device_id_type=MESH)
    for copy in old_copies:
        copy.start()
    b0_a[...] = act_ref[...].T.reshape(b0_a.shape)
    pl.semaphore_wait(barrier, len(greeted))

    def remote(src, dst, send, recv, target):
        return pltpu.make_async_remote_copy(
            src_ref=src, dst_ref=dst, send_sem=send, recv_sem=recv,
            device_id=target, device_id_type=MESH,
        )

    shift = remote(og_ref, gbuf, shift_sem.at[0], shift_sem.at[1], x_down)
    shift.start()

    def z_copy(part, src, slot, dst, dst_slot, target):
        return remote(src, dst, zsend.at[part["i"], slot], zrecv.at[part["i"], dst_slot], target)

    def twin_copy(part, src, dst, slot):
        return remote(src, dst, ocsend.at[part["i"], slot], ocrecv.at[part["i"], slot], twin)

    def z_flows(part):
        cs = part["c"]
        return {
            "own": [
                (zl == 1, z_copy(part, part["own"], 0, part["p"], 0, z_down)),
                (zl == 0, z_copy(part, part["own"], 0, cs[0], 1, z_down)),
                (zl == 0, z_copy(part, part["own"], 6, part["p"], 0, z_up)),
            ],
            "p": [(zl == 0, z_copy(part, part["p"], 1, cs[1], 2, z_down))],
            "c0": [
                (zl == 0, z_copy(part, cs[0], 2, cs[2], 3, z_down)),
                (zl == 1, z_copy(part, cs[0], 2, cs[0], 1, z_down)),
            ],
            "c1": [
                (zl == 0, z_copy(part, cs[1], 3, cs[3], 4, z_down)),
                (zl == 1, z_copy(part, cs[1], 3, cs[1], 2, z_down)),
            ],
            "c2": [(zl == 1, z_copy(part, cs[2], 4, cs[2], 3, z_down))],
            "c3": [(zl == 1, z_copy(part, cs[3], 5, cs[3], 4, z_down))],
        }

    flows = [z_flows(part) for part in parts]

    def z_start(part, name):
        for condition, copy in flows[part["i"]][name]:
            pl.when(condition)(copy.start)

    def y_sends(part, source, dzh, zs):
        far = jnp.where(zs == zl, 0, 2)

        @pl.loop(0, NY)
        def _(yy):
            d = y + NY * dzh - yy

            @pl.when((d >= 1) & (d < dists))
            def _():
                for kk in range(2):
                    piece = part["stage"].at[d - 1, zs, kk]
                    piece[...] = source[assign_ref[d, 2 * zl + kk]]
                    here = (yy == y) & (k == kk)
                    place = part["recv"].at[d, far + jnp.where(k == kk, 0, 1)]
                    done = yrecv.at[part["i"], d]

                    @pl.when(here)
                    def _():
                        pltpu.make_async_copy(piece, place, done).start()

                    @pl.when(jnp.logical_not(here))
                    def _():
                        remote(piece, place, ysend.at[part["i"], d - 1, zs, kk], done,
                               device(x, z, yy, kk)).start()

    def y_send_waits(part):
        @pl.loop(1, dists)
        def _(d):
            yy = lax.rem(y - d + 3 * NY, NY)
            for zs in range(2):
                for kk in range(2):
                    here = (yy == y) & (k == kk)
                    piece = part["stage"].at[d - 1, zs, kk]

                    @pl.when(jnp.logical_not(here))
                    def _():
                        remote(piece, piece, ysend.at[part["i"], d - 1, zs, kk],
                               yrecv.at[part["i"], d], device(x, z, yy, kk)).wait_send()

    def z_wait(part, ref, slot):
        pltpu.make_async_copy(ref, ref, zrecv.at[part["i"], slot]).wait()

    def product(part, strips):
        own = jnp.concatenate(
            [part[n][...].reshape(-1, part[n].shape[2]) for n in ("own", "oc0", "p", "ocp")], axis=1
        )
        return lax.dot_general(
            jnp.concatenate(strips, axis=1), own, (((1,), (1,)), ((), ())),
            preferred_element_type=jnp.float32,
        )

    tokens = 4 * b0_a.shape[2]

    def blend(part, d, fresh):
        old = part["old"]
        old[d] = (
            ema_decay * old[d].astype(jnp.float32) + (1.0 - ema_decay) * (fresh / tokens)
        ).astype(jnp.bfloat16)
        pltpu.make_async_copy(old.at[d], part["out"].at[d], out_sem.at[part["i"], d]).start()

    def compute_first():
        for copy in old_copies:
            copy.wait()
        for part in parts:
            for slot in range(2):
                place = part["oc0"] if slot == 0 else part["ocp"]
                pltpu.make_async_copy(place, place, ocrecv.at[part["i"], slot]).wait()
            a = assign_ref[0, q]
            blend(part, 0, product(part, [part[n][a] for n in ("own", "oc0", "p", "ocp")]))

    def compute(lo, hi):
        @pl.loop(lo, hi)
        def _(d):
            for part in parts:
                got = part["recv"].at[d]
                pltpu.make_async_copy(got, got, yrecv.at[part["i"], d]).wait()
                blend(part, d, product(part, [part["recv"][d, r] for r in range(4)]))

    for part in parts:
        if part["i"] == 1:
            shift.wait_recv()
            b0_g[...] = gbuf[...].T.reshape(b0_g.shape)
        z_start(part, "own")
        twin_copy(part, part["own"], part["oc0"], 0).start()
        y_sends(part, part["own"], 0, zl)
    for part in parts:
        z_wait(part, part["p"], 0)
        z_start(part, "p")
        twin_copy(part, part["p"], part["ocp"], 1).start()
        y_sends(part, part["p"], 0, 1 - zl)
    for n in range(4):
        for part in parts:
            block = part["c"][n]
            z_wait(part, block, n + 1)
            z_start(part, "c%d" % n)
            y_sends(part, block, (n + 2) // 2, n % 2)
        if n == 1:
            compute_first()
        if n == 2:
            compute(1, 3)
    compute(3, dists)

    for part in parts:
        for name in ("own", "p", "c0", "c1", "c2", "c3"):
            for condition, copy in flows[part["i"]][name]:
                pl.when(condition)(copy.wait_send)
        twin_copy(part, part["own"], part["oc0"], 0).wait_send()
        twin_copy(part, part["p"], part["ocp"], 1).wait_send()
        y_send_waits(part)
        for d in range(dists):
            pltpu.make_async_copy(part["old"].at[d], part["out"].at[d], out_sem.at[part["i"], d]).wait()
    shift.wait_send()


def on_device(activations, out_grads, assign, act_old, grad_old):
    tokens, act_width = activations.shape[1:]
    grad_width = out_grads.shape[2]
    dists, act_strip = act_old.shape[1:3]
    grad_strip = grad_old.shape[2]
    bf16 = jnp.bfloat16
    vmem = lambda *shape: pltpu.VMEM(shape, bf16)
    dma = pltpu.SemaphoreType.DMA
    any_spec = pl.BlockSpec(memory_space=pl.ANY)
    act_new, grad_new = pl.pallas_call(
        kernel,
        out_shape=(
            jax.ShapeDtypeStruct(act_old.shape[1:], bf16),
            jax.ShapeDtypeStruct(grad_old.shape[1:], bf16),
        ),
        in_specs=[
            pl.BlockSpec(memory_space=pltpu.VMEM),
            any_spec,
            pl.BlockSpec(memory_space=pltpu.SMEM),
            any_spec,
            any_spec,
        ],
        out_specs=(any_spec, any_spec),
        scratch_shapes=[vmem(4, act_strip, tokens)] * 8
        + [vmem(4, grad_strip, tokens)] * 8
        + [
            vmem(tokens, grad_width),
            vmem(dists - 1, 2, 2, act_strip, tokens),
            vmem(dists - 1, 2, 2, grad_strip, tokens),
            vmem(dists, 4, act_strip, tokens),
            vmem(dists, 4, grad_strip, tokens),
            vmem(*act_old.shape[1:]),
            vmem(*grad_old.shape[1:]),
            dma((2,)),
            dma((2, dists)),
            dma((2,)),
            dma((2, 7)),
            dma((2, 5)),
            dma((2, 2)),
            dma((2, 2)),
            dma((2, dists - 1, 2, 2)),
            dma((2, dists)),
        ],
        compiler_params=pltpu.CompilerParams(
            collective_id=0, has_side_effects=True, vmem_limit_bytes=58 * 1024 * 1024
        ),
        cost_estimate=pl.CostEstimate(
            flops=2 * dists * 4 * tokens * (act_strip * act_width + grad_strip * grad_width),
            bytes_accessed=4 * dists * (act_strip * act_width + grad_strip * grad_width),
            transcendentals=0,
        ),
    )(activations[0], out_grads[0], assign, act_old[0], grad_old[0])
    return act_new[None], grad_new[None]


def solution(mesh):
    return jax.shard_map(
        on_device,
        mesh=mesh,
        in_specs=(
            P("section", "dist", "col"),
            P("section", "dist", "col"),
            P(),
            P("section", None, "dist", "col"),
            P("section", None, "dist", "col"),
        ),
        out_specs=(P("section", None, "dist", "col"), P("section", None, "dist", "col")),
        check_vma=False,
    )
```

time: 559 us -> 110 us (0.20)
  the two profiles are of different devices: /device:TPU:247 before, /device:TPU:29 now
where the time goes in v1:
time: 110 us
  Pallas kernels  103 us (94%)
  local copies, waits for them, and re-layouts  6.6 us (6%)
    pallas_call x1, Pallas kernels, on_device(): pl.pallas_call(kernel, out_shape=(jax.ShapeDtypeStruct(act_old.shape[1:],...  103 us
    unnamed x5, local copies, waits for them, and re-layouts  6.6 us

profile of v1, /device:TPU:29, one launch (start us, length us, event | category | flops | bytes accessed | tf_op | source)
XLA Modules:
  0.0 110.2 jit_solution(11435529593686942091)
XLA Ops:
  0.6 1.4 %copy.7.assign_ref = s32[9,4]{1,0:T(8,128)} copy(s32[9,4]{0,1:T(4,128)} %param.7) | data formatting | bytes 288 | tf_op args[2]
  2.0 103.0 %shard_map.68 = (bf16[9,224,896]{2,1,0:T(8,128)(2,1)}, bf16[9,128,512]{2,1,0:T(8,128)(2,1)}) custom-call(bf16[256,896]{1,0:T(8,128)(2,1)} %bitcast.10, bf16[256,512]{1,0:T(8,128)(2,1)} %bitcast.11, s32[9,4]{1,0:T(8,128)} %copy.7.assign_ref, bf16[9,224,896]{2,1,0:T(8,128)(2,1)} %bitcast.8, bf16[9,128,512]{2,1,0:T(8,128)(2,1)} %bitcast.9), custom_call_target="tpu_custom_call" | custom-call | flops 4907335680 | bytes 9584640 | tf_op jit(solution)/shard_map/pallas_call | solution.py:228
  105.0 0.0 copy-start
  105.0 4.2 %copy.10 = bf16[1,9,224,896]{3,2,1,0:T(8,128)(2,1)} copy(bf16[1,9,224,896]{3,2,1,0:T(8,128)(2,1)} %bitcast.6) | data formatting | bytes 7225344
  109.2 0.0 copy-done
  109.2 1.0 copy.11
Async XLA Ops:
  105.0 4.2 %copy-start = (bf16[9,128,512]{2,1,0:T(8,128)(2,1)S(1)}, bf16[9,128,512]{2,1,0:T(8,128)(2,1)}, u32[]{:S(2)}) copy-start(bf16[9,128,512]{2,1,0:T(8,128)(2,1)} %get-tuple-element.5) | copy-start | bytes 3538948

commit v2 on v1

v2 whole, which is shorter than its diff:
```python
import jax
import jax.numpy as jnp
from jax import lax
from jax.experimental import pallas as pl
from jax.experimental.pallas import tpu as pltpu
from jax.sharding import PartitionSpec as P

ema_decay = 0.75
MESH = pl.DeviceIdType.MESH
NY = 4
NZ = 8
NX = 4


NAMES = ("own", "p", "c0", "c1", "c2", "c3", "oc0", "ocp")
ACT_PARTS, GRAD_PARTS = 4, 2
HALVES = 2
SAME = ("own", "oc0", "p", "ocp")


STEPS = (
    (
        (("own",), ("p",), ("c0", "c3"), ("c2", "c1"), ()),
        (("own",), ("p",), ("c0",), ("c1",), ("c3", "c2")),
    ),
    ((("own",), ("c0", "p"), ("c1",), ("c2",), ("c3",)),) * 2,
)
FIRST = (0,0,1,2,3,3)


def arrivals(parity):
    for step in range(len(STEPS[0][0]) + max(FIRST)):
        for i, first in enumerate(FIRST):
            steps = STEPS[parity][0 if i < ACT_PARTS else 1]
            if 0 <= step - first < len(steps):
                for name in steps[step - first]:
                    yield i, name


def kernel(act_ref, og_ref, assign_hbm, olda_hbm, oldg_hbm, olda, oldg, *scratch):
    scratch = list(scratch)
    parts = []
    for i in range(ACT_PARTS + GRAD_PARTS):
        part = {name: scratch.pop(0) for name in NAMES}
        part.update(i=i, act=i < ACT_PARTS, stage=scratch.pop(0))
        parts.append(part)
    (recv_a, recv_g, gbuf, assign_ref, assign_sem,
     old_sem, shift_sem, zsend, zrecv, ocsend, ocrecv, ysend, yrecv) = scratch
    x = lax.axis_index("section")
    c = lax.axis_index("col")
    q = lax.axis_index("dist")
    y, zh = lax.rem(c, NY), c // NY
    zl, k = q // 2, lax.rem(q, 2)
    z = 2 * zh + zl
    dists = olda.shape[0]
    for part in parts:
        kind = 0 if part["act"] else 1
        part.update(kind=kind, recv=(recv_a, recv_g)[kind], n=part["i"] - kind * ACT_PARTS)
    acts, grads = parts[:ACT_PARTS], parts[ACT_PARTS:]
    kinds = tuple(
        dict(i=i, old=old, recv=(recv_a, recv_g)[i], halves=[own[h::HALVES] for h in range(HALVES)])
        for i, own, old in ((0, acts, olda), (1, grads, oldg))
    )

    def device(xx, zz, yy, kk):
        return (xx, (zz // 2) * NY + yy, lax.rem(zz, 2) * 2 + kk)

    z_down = device(x, lax.rem(z + NZ - 1, NZ), y, k)
    z_up = device(x, lax.rem(z + 1, NZ), y, k)
    z_far = device(x, lax.rem(z + 3, NZ), y, k)
    z_back = device(x, lax.rem(z + NZ - 3, NZ), y, k)
    twin = device(x, z, y, 1 - k)
    x_down = device(lax.rem(x + NX - 1, NX), z, y, k)
    x_up = device(lax.rem(x + 1, NX), z, y, k)

    old_copies = [
        pltpu.make_async_copy(olda_hbm, olda, old_sem.at[0]),
        pltpu.make_async_copy(oldg_hbm, oldg, old_sem.at[1]),
    ]
    assign_copy = pltpu.make_async_copy(assign_hbm, assign_ref, assign_sem)

    barrier = pltpu.get_barrier_semaphore()
    greeted = [z_down, z_up, z_far, z_back, twin, x_down, x_up]
    for step in range(1, NY):
        for kk in range(2):
            greeted.append(device(x, z, lax.rem(y + step, NY), kk))
    for other in greeted:
        pl.semaphore_signal(barrier, inc=1, device_id=other, device_id_type=MESH)
    assign_copy.start()
    for copy in old_copies:
        copy.start()
    lanes = act_ref.shape[0] // HALVES

    def place_own(kind, rows_ref):
        for h, members in enumerate(kind["halves"]):
            turned = rows_ref[pl.ds(h * lanes, lanes), :].T.reshape(4, -1, lanes)
            height = turned.shape[1] // len(members)
            for r, part in enumerate(members):
                part["own"][...] = turned[:, r * height:(r + 1) * height]

    place_own(kinds[0], act_ref)
    assign_copy.wait()
    pl.semaphore_wait(barrier, len(greeted))

    def remote(src, dst, send, recv, target):
        return pltpu.make_async_remote_copy(
            src_ref=src, dst_ref=dst, send_sem=send, recv_sem=recv,
            device_id=target, device_id_type=MESH,
        )

    shift = remote(og_ref, gbuf, shift_sem.at[0], shift_sem.at[1], x_down)
    shift.start()

    def z_copy(part, src, slot, dst, dst_slot, target):
        return remote(src, dst, zsend.at[part["i"], slot], zrecv.at[part["i"], dst_slot], target)

    def twin_copy(part, src, dst, slot):
        return remote(src, dst, ocsend.at[part["i"], slot], ocrecv.at[part["i"], slot], twin)

    def z_flows(part):
        cs = tuple(part["c%d" % n] for n in range(4))
        flows = {
            "own": [
                (1, z_copy(part, part["own"], 0, part["p"], 0, z_down)),
                (0, z_copy(part, part["own"], 0, cs[0], 1, z_down)),
                (0, z_copy(part, part["own"], 6, part["p"], 0, z_up)),
                (1, z_copy(part, part["own"], 6, cs[3], 4, z_far)),
            ],
            "p": [(0, z_copy(part, part["p"], 1, cs[1], 2, z_down))],
            "c0": [
                (0, z_copy(part, cs[0], 2, cs[2], 3, z_down)),
                (1, z_copy(part, cs[0], 2, cs[0], 1, z_down)),
            ],
            "c1": [(1, z_copy(part, cs[1], 3, cs[1], 2, z_down))],
            "c2": [],
            "c3": [],
        }
        if part["act"]:
            flows["p"].append((1, z_copy(part, part["p"], 7, cs[2], 3, z_far)))
            flows["c3"].append((0, z_copy(part, cs[3], 7, cs[3], 4, z_up)))
        else:
            flows["c1"].append((0, z_copy(part, cs[1], 3, cs[3], 4, z_down)))
            flows["c2"].append((1, z_copy(part, cs[2], 4, cs[2], 3, z_down)))
        return flows

    flows = [z_flows(part) for part in parts]

    def z_start(part, name, parity):
        for wanted, copy in flows[part["i"]][name]:
            if wanted == parity:
                copy.start()

    columns = [zh * NY + jnp.where(y + r >= NY, y + r - NY, y + r) for r in range(NY)]

    def y_sends(part, source, parity, dzh, zs):
        for r in range(NY):
            if dzh == 0 and r == 0:
                continue
            d = c + NY * dzh - columns[r]

            def send():
                for other in range(2):
                    kk = 1 - k if other else k
                    piece = part["stage"].at[d - 1, zs, other]
                    piece[...] = source[assign_ref[2 * parity + kk, d]]
                    place = part["recv"].at[d, part["n"], 2 * (zs != parity) + other]
                    done = yrecv.at[part["kind"], d]
                    if r == 0 and other == 0:
                        pltpu.make_async_copy(piece, place, done).start()
                    else:
                        remote(piece, place, ysend.at[part["i"]], done,
                               (x, columns[r], 2 * parity + kk)).start()

            if dzh == 1 or r == 0:
                send()
            else:
                pl.when(d >= 1 if dzh == 0 else d < dists)(send)

    def y_send_wait(part):
        sent = part["stage"].at[pl.ds(0, dists - 2)]
        pltpu.make_async_copy(sent, sent, ysend.at[part["i"]]).wait()

    def z_wait(part, ref, slot):
        pltpu.make_async_copy(ref, ref, zrecv.at[part["i"], slot]).wait()

    def product(kind, strips_of):
        own = jnp.concatenate([
            jnp.concatenate([p[n][a] for a in range(4) for p in members], axis=0)
            for members in kind["halves"] for n in SAME
        ], axis=1)
        strips = jnp.concatenate([
            jnp.concatenate(strips_of(members, slot), axis=0)
            for members in kind["halves"] for slot in range(len(SAME))
        ], axis=1)
        return lax.dot_general(
            strips, own, (((1,), (1,)), ((), ())), preferred_element_type=jnp.float32
        )

    tokens = 4 * act_ref.shape[0]

    def blend(kind, d, fresh):
        old = kind["old"]
        old[d] = (
            ema_decay * old[d].astype(jnp.float32) + (1.0 - ema_decay) * (fresh / tokens)
        ).astype(jnp.bfloat16)

    def compute_first(kind):
        old_copies[kind["i"]].wait()
        for part in sum(kind["halves"], []):
            for slot in range(2):
                place = part["oc0"] if slot == 0 else part["ocp"]
                pltpu.make_async_copy(place, place, ocrecv.at[part["i"], slot]).wait()
        a = assign_ref[q, 0]
        blend(kind, 0, product(kind, lambda members, slot: [p[SAME[slot]][a] for p in members]))

    count = 2

    def compute(kind, lo, hi):
        @pl.loop(lo, hi)
        def _(group):
            members = [group * count + 1 + n for n in range(count)]
            for d in members:
                got = kind["recv"].at[d]
                pltpu.make_async_copy(got, got, yrecv.at[kind["i"], d]).wait()
            fresh = product(
                kind, lambda those, slot: [p["recv"][d, p["n"], slot] for d in members for p in those]
            )
            height = fresh.shape[0] // count
            for n, d in enumerate(members):
                blend(kind, d, fresh[n * height:(n + 1) * height])

    def arrived(i, name, parity):
        part = parts[i]
        if name == "own":
            if i == ACT_PARTS:
                shift.wait_recv()
                place_own(kinds[1], gbuf)
            z_start(part, "own", parity)
            twin_copy(part, part["own"], part["oc0"], 0).start()
            y_sends(part, part["own"], parity, 0, parity)
        elif name == "p":
            z_wait(part, part["p"], 0)
            z_start(part, "p", parity)
            twin_copy(part, part["p"], part["ocp"], 1).start()
            y_sends(part, part["p"], parity, 0, 1 - parity)
        else:
            n = int(name[1])
            z_wait(part, part[name], n + 1)
            z_start(part, name, parity)
            y_sends(part, part[name], parity, (n + 2) // 2, n % 2)

    for parity in range(2):

        @pl.when(zl == parity)
        def _():
            for i, name in arrivals(parity):
                arrived(i, name, parity)

    groups = (dists - 1) // count
    compute_first(kinds[0])
    compute(kinds[0], 0, groups)
    compute_first(kinds[1])
    for parity in range(2):

        @pl.when(zl == parity)
        def _():
            for part in parts:
                for name in NAMES[:6]:
                    for wanted, copy in flows[part["i"]][name]:
                        if wanted == parity:
                            copy.wait_send()

    for part in parts:
        twin_copy(part, part["own"], part["oc0"], 0).wait_send()
        twin_copy(part, part["p"], part["ocp"], 1).wait_send()
    compute(kinds[1], 0, groups)
    for part in parts:
        y_send_wait(part)
    shift.wait_send()


def on_device(activations, out_grads, assign, act_old, grad_old):
    tokens, act_width = activations.shape[1:]
    grad_width = out_grads.shape[2]
    dists, act_strip = act_old.shape[1:3]
    grad_strip = grad_old.shape[2]
    bf16 = jnp.bfloat16
    vmem = lambda *shape: pltpu.VMEM(shape, bf16)
    dma = pltpu.SemaphoreType.DMA
    half = tokens // HALVES
    count = ACT_PARTS + GRAD_PARTS
    any_spec = pl.BlockSpec(memory_space=pl.ANY)
    vmem_spec = pl.BlockSpec(memory_space=pltpu.VMEM)
    act_new, grad_new = pl.pallas_call(
        kernel,
        out_shape=(
            vmem(*act_old.shape[1:]),
            vmem(*grad_old.shape[1:]),
        ),
        in_specs=[
            vmem_spec,
            any_spec,
            any_spec,
            any_spec,
            any_spec,
        ],
        out_specs=(vmem_spec, vmem_spec),
        scratch_shapes=[
            vmem(*shape)
            for rows, lanes in ((act_strip * HALVES // ACT_PARTS, half),) * ACT_PARTS
            + ((grad_strip * HALVES // GRAD_PARTS, half),) * GRAD_PARTS
            for shape in [(4, rows, lanes)] * len(NAMES)
            + [(dists - 1, 2, 2, rows, lanes)]
        ]
        + [
            vmem(dists, ACT_PARTS, 4, act_strip * HALVES // ACT_PARTS, half),
            vmem(dists, GRAD_PARTS, 4, grad_strip * HALVES // GRAD_PARTS, half),
            vmem(tokens, grad_width),
            pltpu.SMEM(assign.shape[::-1], jnp.int32),
            dma,
            dma((2,)),
            dma((2,)),
            dma((count, 8)),
            dma((count, 5)),
            dma((count, 2)),
            dma((count, 2)),
            dma((count,)),
            dma((2, dists)),
        ],
        compiler_params=pltpu.CompilerParams(
            collective_id=0, has_side_effects=True, vmem_limit_bytes=57 * 1024 * 1024
        ),
        cost_estimate=pl.CostEstimate(
            flops=2 * dists * 4 * tokens * (act_strip * act_width + grad_strip * grad_width),
            bytes_accessed=4 * dists * (act_strip * act_width + grad_strip * grad_width),
            transcendentals=0,
        ),
    )(activations[0], out_grads[0], assign.T, act_old[0], grad_old[0])
    return act_new[None], grad_new[None]


def solution(mesh):
    return jax.shard_map(
        on_device,
        mesh=mesh,
        in_specs=(
            P("section", "dist", "col"),
            P("section", "dist", "col"),
            P(),
            P("section", None, "dist", "col"),
            P("section", None, "dist", "col"),
        ),
        out_specs=(P("section", None, "dist", "col"), P("section", None, "dist", "col")),
        check_vma=False,
    )
```

time: 110 us -> 89.1 us (0.81)
  the two profiles are of different devices: /device:TPU:29 before, /device:TPU:247 now
where the time goes in v2:
time: 89.1 us; the launch traced here: 88.9 us
  Pallas kernels  85.5 us (96%)
  local copies, waits for them, and re-layouts  2.83 us (3%)
    pallas_call x1, Pallas kernels, on_device(): pl.pallas_call(kernel, out_shape=(vmem(*act_old.shape[1:]), vmem(*grad_ol...  85.5 us
    unnamed x2, local copies, waits for them, and re-layouts  2.83 us

profile of v2, /device:TPU:247, one launch (start us, length us, event | category | flops | bytes accessed | tf_op | source)
XLA Modules:
  0.0 88.9 jit_solution(4018492001338997272)
XLA Ops:
  0.6 85.5 %shard_map.68 = (bf16[9,224,896]{2,1,0:T(8,128)(2,1)S(1)}, bf16[9,128,512]{2,1,0:T(8,128)(2,1)S(1)}) custom-call(bf16[256,896]{1,0:T(8,128)(2,1)} %bitcast.11, bf16[256,512]{1,0:T(8,128)(2,1)} %bitcast.12, s32[4,9]{1,0:T(4,128)} %bitcast.13, bf16[9,224,896]{2,1,0:T(8,128)(2,1)} %bitcast.9, bf16[9,128,512]{2,1,0:T(8,128)(2,1)} %bitcast.10), custom_call_target="tpu_custom_call" | custom-call | flops 4907335680 | bytes 9584640 | tf_op jit(solution)/shard_map/pallas_call | solution.py:294
  86.1 1.8 %copy.9 = bf16[1,9,224,896]{3,2,1,0:T(8,128)(2,1)} copy(bf16[1,9,224,896]{3,2,1,0:T(8,128)(2,1)S(1)} %bitcast.7) | data formatting | bytes 7225344
  87.9 1.0 %copy.10 = bf16[1,9,128,512]{3,2,1,0:T(8,128)(2,1)} copy(bf16[1,9,128,512]{3,2,1,0:T(8,128)(2,1)S(1)} %bitcast.8) | data formatting | bytes 2359296

commit v3 on v2

--- a/solution.py
+++ b/solution.py
@@ -153,7 +153,7 @@
     columns = [zh * NY + jnp.where(y + r >= NY, y + r - NY, y + r) for r in range(NY)]
 
     def y_sends(part, source, parity, dzh, zs):
-        for r in range(NY):
+        for r in (2, 1, 3, 0):
             if dzh == 0 and r == 0:
                 continue
             d = c + NY * dzh - columns[r]
@@ -254,12 +254,13 @@
         @pl.when(zl == parity)
         def _():
             for i, name in arrivals(parity):
+                if (i, name) == (len(parts) - 1, "c2" if parity == 0 else "c3"):
+                    for kind in kinds:
+                        compute_first(kind)
                 arrived(i, name, parity)
 
     groups = (dists - 1) // count
-    compute_first(kinds[0])
     compute(kinds[0], 0, groups)
-    compute_first(kinds[1])
     for parity in range(2):
 
         @pl.when(zl == parity)

time: 89.1 us -> 88.7 us (level)
  no operation moved by 1% of the time
where the time goes in v3:
time: 88.7 us; the launch traced here: 88.2 us
  Pallas kernels  84.7 us (95%)
  local copies, waits for them, and re-layouts  2.83 us (3%)
    pallas_call x1, Pallas kernels, on_device(): pl.pallas_call(kernel, out_shape=(vmem(*act_old.shape[1:]), vmem(*grad_ol...  84.7 us
    unnamed x2, local copies, waits for them, and re-layouts  2.83 us

profile of v3, /device:TPU:247, one launch (start us, length us, event | category | flops | bytes accessed | tf_op | source)
XLA Modules:
  0.0 88.2 jit_solution(4594973754249254039)
XLA Ops:
  0.6 84.7 %shard_map.68 = (bf16[9,224,896]{2,1,0:T(8,128)(2,1)S(1)}, bf16[9,128,512]{2,1,0:T(8,128)(2,1)S(1)}) custom-call(bf16[256,896]{1,0:T(8,128)(2,1)} %bitcast.11, bf16[256,512]{1,0:T(8,128)(2,1)} %bitcast.12, s32[4,9]{1,0:T(4,128)} %bitcast.13, bf16[9,224,896]{2,1,0:T(8,128)(2,1)} %bitcast.9, bf16[9,128,512]{2,1,0:T(8,128)(2,1)} %bitcast.10), custom_call_target="tpu_custom_call" | custom-call | flops 4907335680 | bytes 9584640 | tf_op jit(solution)/shard_map/pallas_call | solution.py:295
  85.4 1.8 %copy.9 = bf16[1,9,224,896]{3,2,1,0:T(8,128)(2,1)} copy(bf16[1,9,224,896]{3,2,1,0:T(8,128)(2,1)S(1)} %bitcast.7) | data formatting | bytes 7225344
  87.2 1.0 %copy.10 = bf16[1,9,128,512]{3,2,1,0:T(8,128)(2,1)} copy(bf16[1,9,128,512]{3,2,1,0:T(8,128)(2,1)S(1)} %bitcast.8) | data formatting | bytes 2359296
